TPU v7x, 32 devices: a whole 2x2x4 slice. The times are simulated.
32 devices in a mesh: grp: 2 (over x), gx: 16 (over z, y, core).
Axes of the slice: x: 2, y: 2, z: 4, core: 2. Of those that a mesh axis runs over, the one named last changes fastest.
Arguments:
- hidden_state: bfloat16 [32, 16384], P('grp', 'gx'), parts along dimension 0, may hold values from -120 to 120
- norm_gain: bfloat16 [16384], P('gx'), may hold values from 0.099609375 to 1.8984375
- w_query: bfloat16 [16384, 16384], P('gx'), may hold values from -0.0625 to 0.0625
- w_key: bfloat16 [16384, 1024], P('gx'), may hold values from -0.046875 to 0.046875
- w_value: bfloat16 [16384, 1024], P('gx'), may hold values from -0.046875 to 0.046875
- w_out: bfloat16 [16384, 16384], P(None, 'gx'), may hold values from -0.25 to 0.25
- cache_keys: bfloat16 [32, 512, 1024], P('grp', 'gx'), parts along dimension 0, may hold values from -384 to 384
- cache_values: bfloat16 [32, 512, 1024], P('grp', 'gx'), parts along dimension 0, may hold values from -6 to 6
- lengths: int32 [32], P('grp'), parts along dimension 0, may hold values from 1 to 512, 4096 in all
Outputs:
- attention_out: bfloat16 [32, 16384], P('grp', 'gx'), parts along dimension 0
- new_entries: bfloat16 [2, 32, 1024], P(None, 'grp'), parts along dimension 1
There are 2 independent parts, one for each index of `grp`. A program takes and returns all parts, laid end to end along the dimension named above; an argument that names none is the same for every part. Nothing has to cross between parts.
All inputs are finite; a program needn't handle non-finite values.
Results may differ from a plain program's by a relative error of at most 0.004.
The roundings to bfloat16 on the way count: a program that leaves them out, or rounds other values in their place, can miss the bound.
Values may be sent and summed in bfloat16 or wider, within the bound.
A program may use at most 192 MiB of HBM per device.

v0:
```python
import math

import jax
import jax.numpy as jnp
from jax import lax
from jax.sharding import PartitionSpec as P

D = 16384
H = 128
KV = 8
HD = 128


EPS = 1e-05
BASE = 500000.0


def rotate(values, positions):
    row_count = values.shape[0]
    head_count = values.shape[1] // HD
    half_dim = HD // 2
    shaped = values.reshape(row_count, head_count, HD)
    frequency = jnp.exp(jnp.arange(half_dim, dtype=jnp.float32) * (-2.0 * math.log(BASE) / HD))
    angles = positions.astype(jnp.float32)[:, None, None] * frequency[None, None, :]
    cos_table = jnp.cos(angles)
    sin_table = jnp.sin(angles)
    leading = shaped[:, :, :half_dim]
    trailing = shaped[:, :, half_dim:]
    turned = jnp.concatenate(
        [leading * cos_table - trailing * sin_table, trailing * cos_table + leading * sin_table],
        axis=-1,
    )
    return turned.reshape(row_count, head_count * HD)


def finish(mix_part, total_part, own_weight, own_value, row_count):
    heads_here = total_part.shape[1]
    mixed = mix_part.reshape(row_count, heads_here, HD) + own_weight[:, :, None] * own_value
    head_out = mixed / (total_part + own_weight)[:, :, None]
    return head_out.reshape(row_count, heads_here * HD).astype(jnp.bfloat16)


def on_device(
    hidden_state, norm_gain, w_query, w_key, w_value, w_out, cache_keys, cache_values, lengths
):
    tile_count = lax.axis_size("gx")
    device_slot = lax.axis_index("gx")
    row_count = hidden_state.shape[0]
    group_size = H // KV
    local_heads = H // tile_count
    scale_factor = HD ** (-0.5)
    widened = hidden_state.astype(jnp.float32)
    squares = jnp.sum(widened * widened, axis=1, keepdims=True)
    scaled = (widened * norm_gain.astype(jnp.float32)[None, :]).astype(jnp.bfloat16)
    part_query = jnp.dot(scaled, w_query, preferred_element_type=jnp.float32)
    part_key = jnp.dot(scaled, w_key, preferred_element_type=jnp.float32)
    part_value = jnp.dot(scaled, w_value, preferred_element_type=jnp.float32)
    query_sum, key_sum, value_sum, square_sum = lax.psum(
        (part_query, part_key, part_value, squares), "gx"
    )
    inv_rms = lax.rsqrt(square_sum / D + EPS)
    queries = rotate(inv_rms * query_sum, lengths).astype(jnp.bfloat16)
    new_key = rotate(inv_rms * key_sum, lengths).astype(jnp.bfloat16)
    new_value = (inv_rms * value_sum).astype(jnp.bfloat16)
    slot_count = cache_keys.shape[1]
    positions = device_slot * slot_count + jnp.arange(slot_count, dtype=jnp.int32)
    valid_mask = positions[None, :] < lengths[:, None]
    grouped_query = queries.reshape(row_count, KV, group_size, HD)
    key_block = cache_keys.reshape(row_count, slot_count, KV, HD)
    scores = jnp.einsum(
        "rkgd,rpkd->rpkg", grouped_query, key_block, preferred_element_type=jnp.float32
    )
    scores = scores.reshape(row_count, slot_count, H) * scale_factor
    scores = jnp.where(valid_mask[:, :, None], scores, -1e30)
    own_score = jnp.einsum(
        "rkgd,rkd->rkg",
        grouped_query,
        new_key.reshape(row_count, KV, HD),
        preferred_element_type=jnp.float32,
    )
    own_score = own_score.reshape(row_count, H) * scale_factor
    block_peak = jnp.max(scores, axis=1)
    weights = jnp.where(valid_mask[:, :, None], jnp.exp(scores - block_peak[:, None, :]), 0.0)
    partial_total = jnp.sum(weights, axis=1)
    rounded = weights.astype(jnp.bfloat16).reshape(row_count, slot_count, KV, group_size)
    value_block = cache_values.reshape(row_count, slot_count, KV, HD)
    partial_mix = jnp.einsum(
        "rpkg,rpkd->rkgd", rounded, value_block, preferred_element_type=jnp.float32
    )
    partial_mix = partial_mix.reshape(row_count, H, HD)
    own_value = jnp.broadcast_to(
        new_value.astype(jnp.float32).reshape(row_count, KV, 1, HD), (row_count, KV, group_size, HD)
    )
    own_value = own_value.reshape(row_count, H, HD)
    first_head = device_slot * local_heads
    score_peak = lax.pmax(jnp.maximum(block_peak, own_score), "gx")
    rescale = jnp.exp(block_peak - score_peak)
    scaled_mix = (rescale[:, :, None] * partial_mix).reshape(row_count, H * HD)
    scaled_total = rescale * partial_total
    own_weight = jnp.exp(own_score - score_peak)
    mix_share, total_share = (
        lax.psum_scatter(scaled_mix, "gx", scatter_dimension=1, tiled=True),
        lax.psum_scatter(scaled_total, "gx", scatter_dimension=1, tiled=True),
    )
    weight_mine = lax.dynamic_slice_in_dim(own_weight, first_head, local_heads, 1)
    value_mine = lax.dynamic_slice_in_dim(own_value, first_head, local_heads, 1)
    head_out = finish(mix_share, total_share, weight_mine, value_mine, row_count)
    result = jnp.dot(
        lax.all_gather(head_out, "gx", axis=1, tiled=True),
        w_out,
        preferred_element_type=jnp.float32,
    )
    return (result.astype(jnp.bfloat16), jnp.stack([new_key, new_value]))


def solution(mesh):
    return jax.shard_map(
        on_device,
        mesh=mesh,
        in_specs=(
            P("grp", "gx"),
            P("gx"),
            P("gx", None),
            P("gx", None),
            P("gx", None),
            P(None, "gx"),
            P("grp", "gx", None),
            P("grp", "gx", None),
            P("grp"),
        ),
        out_specs=(P("grp", "gx"), P(None, "grp", None)),
        check_vma=False,
    )
```

profile of v0, /device:TPU:0, one launch (start us, length us, event | category | flops | bytes accessed | tf_op | source)
XLA Modules:
  0.0 266.7 jit_solution(4844727590568705023)
XLA Ops:
  7.2 0.0 copy-start
  7.2 0.0 copy-start.5
  7.2 0.0 copy-start.3
  7.2 0.0 all-reduce.4.cloned.1.call-start
  7.3 0.8 convert_element_type.50
  8.1 16.5 %fusion.23 = f32[16,16384]{1,0:T(8,128)} fusion(bf16[1024,16384]{1,0:T(8,128)(2,1)} %param.11, bf16[16,1024]{1,0:T(8,128)(2,1)} %param.9, f32[1024]{0:T(1024)S(1)} %convert_element_type.50), kind=kOutput, calls=%fused_computation.40 | convolution fusion | flops 536920064 | bytes 34639872 | tf_op jit(solution)/shard_map/dot_general | solution.py:55
  24.6 0.0 copy-done.3
  24.6 1.0 fusion.21
  25.6 0.0 copy-done.1
  25.6 1.0 fusion.19
  26.6 0.0 all-reduce.4.cloned.1.call-update
  26.6 0.0 reduce-scatter.3.cloned.1.call-start
  26.7 0.1 fusion.13
  26.8 35.1 %psum.28 = f32[16,1]{0,1:T(1,128)S(1)} all-reduce(f32[16,1]{0,1:T(1,128)S(1)} %bitcast.78), channel_id=1, replica_groups=mesh['grp'=2,'gx'=16] {'gx'}, use_global_device_ids=true, to_apply=%region_1.0 | all-reduce | flops 16 | bytes 128 | tf_op jit(solution)/shard_map/psum | solution.py:58
  61.9 0.0 copy-done.4
  62.0 0.1 broadcast_compare_fusion
  62.1 0.1 multiply_cosine_fusion
  62.2 61.3 %all-reduce.4.cloned.1.call-done = (f32[16,16384]{1,0:T(8,128)}, f32[16,1024]{1,0:T(8,128)}, f32[16,1024]{1,0:T(8,128)}) async-done(((f32[16,16384]{1,0:T(8,128)}, f32[16,1024]{1,0:T(8,128)}, f32[16,1024]{1,0:T(8,128)}), (f32[16,16384]{1,0:T(8,128)}, f32[16,1024]{1,0:T(8,128)}, f32[16,1024]{1,0:T(8,128)})) %all-reduce.4.cloned.1.call-update) | async-done | bytes 1179664 | tf_op jit(solution)/shard_map/psum | solution.py:58
  123.5 1.4 multiply_bitcast_fusion
  124.9 0.2 copy.21
  125.1 0.5 subtract_convert_fusion
  125.6 0.3 pad_maximum_fusion
  125.9 0.8 copy-done.2
  126.7 2.0 fusion.30
  128.7 0.1 reduce_max.12
  128.8 0.7 fusion.7
  129.5 2.7 %fusion.2 = f32[16,8,16,128]{3,2,1,0:T(8,128)} fusion(f32[16,32,8,16]{1,3,2,0:T(8,128)S(1)} %get-tuple-element.19, f32[16,8,16]{2,1,0:T(8,128)S(1)} %get-tuple-element.18, pred[16,32]{1,0:T(8,128)(4,1)S(1)} %broadcast_compare_fusion, bf16[16,32,1024]{2,1,0:T(8,128)(2,1)} %param.16), kind=kOutput, calls=%fused_computation.5 | convolution fusion | flops 16973824 | bytes 2368000 | tf_op jit(solution)/shard_map/rpkg,rpkd->rkgd/dot_general | solution.py:87
  132.2 0.1 reduce_sum.22
  132.3 1.0 fusion.27
  133.2 0.1 multiply_subtract_fusion
  133.3 0.1 fusion.38
  133.4 1.4 fusion.17
  134.9 0.1 mul.203
  135.0 30.8 %pmax.7 = f32[16,128]{1,0:T(8,128)S(1)} all-reduce(f32[16,128]{1,0:T(8,128)S(1)} %max.5), channel_id=1, replica_groups=mesh['grp'=2,'gx'=16] {'gx'}, use_global_device_ids=true, to_apply=%region_5.6 | all-reduce | flops 2048 | bytes 16384 | tf_op jit(solution)/shard_map/pmax | solution.py:96
  165.8 0.3 mul.204
  166.1 3.4 %bitcast_multiply_fusion = f32[16,16384]{1,0:T(8,128)} fusion(f32[2,8,128,128]{3,2,1,0:T(8,128)} %bitcast.68, f32[2,8,128,128]{3,2,1,0:T(8,128)S(1)} %bitcast.67), kind=kLoop, calls=%fused_computation.4 | loop fusion | flops 262144 | bytes 3145728 | tf_op jit(solution)/shard_map/mul | solution.py:98
  169.5 0.0 reduce-scatter.3.cloned.1.call-update
  169.6 0.6 dynamic-slice
  170.8 0.1 maximum_convert_fusion
  170.9 30.1 %all-reduce = f32[16,128]{1,0:T(8,128)S(1)} all-reduce(f32[16,128]{1,0:T(8,128)S(1)} %get-tuple-element.7), channel_id=3, replica_groups=mesh['grp'=2,'gx'=16] {'gx'}, use_global_device_ids=true, to_apply=%region_9.10.clone | all-reduce | flops 2048 | bytes 16384
  201.1 0.1 dynamic-slice_add_fusion
  201.1 0.6 pad_maximum_fusion.1
  201.8 22.6 %reduce-scatter.3.cloned.1.call-done = f32[16,1024]{1,0:T(8,128)} async-done(((f32[16,16384]{1,0:T(8,128)}), f32[16,1024]{1,0:T(8,128)}) %reduce-scatter.3.cloned.1.call-update) | async-done | bytes 65552 | tf_op jit(solution)/shard_map/reduce_scatter | solution.py:102
  224.4 0.9 copy.25
  225.2 0.1 broadcast_in_dim.53
  225.3 0.1 fusion.16
  225.4 21.0 %all_gather.3 = bf16[16,16384]{1,0:T(8,128)(2,1)S(1)} all-gather(bf16[16,1024]{1,0:T(8,128)(2,1)S(1)} %bitcast.74), channel_id=1, replica_groups=mesh['grp'=2,'gx'=16] {'gx'}, dimensions={1}, use_global_device_ids=true | all-gather | bytes 557056 | tf_op jit(solution)/shard_map/all_gather | solution.py:109
  246.4 13.4 %convolution_convert_fusion = bf16[16,1024]{1,0:T(8,128)(2,1)} fusion(bf16[16,16384]{1,0:T(8,128)(2,1)S(1)} %all_gather.3, bf16[16384,1024]{1,0:T(8,128)(2,1)} %param.14), kind=kOutput, calls=%fused_computation.3 | convolution fusion | flops 536887296 | bytes 34111488 | tf_op jit(solution)/shard_map/dot_general | solution.py:108
  (16 shorter events, 0.1 us)
Async XLA Ops:
  7.2 17.4 %copy-start = (bf16[1024,1024]{1,0:T(8,128)(2,1)S(1)}, bf16[1024,1024]{1,0:T(8,128)(2,1)}, u32[]{:S(2)}) copy-start(bf16[1024,1024]{1,0:T(8,128)(2,1)} %param.12) | copy-start | bytes 6291460
  7.2 162.4 %copy-start.5 = (u32[32]{0:T(128)S(1)}, u32[32]{0:T(128)}, u32[]{:S(2)}) copy-start(u32[32]{0:T(128)} %constant.30) | copy-start | bytes 388
  7.2 17.4 %copy-start.3 = (bf16[16,1024]{1,0:T(8,128)(2,1)S(1)}, bf16[16,1024]{1,0:T(8,128)(2,1)}, u32[]{:S(2)}) copy-start(bf16[16,1024]{1,0:T(8,128)(2,1)} %param.9) | copy-start | bytes 98308
  7.2 54.7 %copy-start.4 = (s32[16]{0:T(128)S(1)}, s32[16]{0:T(128)}, u32[]{:S(2)}) copy-start(s32[16]{0:T(128)} %param.17) | copy-start | bytes 196
  7.2 116.3 %all-reduce.4.cloned.1.call-start = ((), (), s32[]{:S(2)}) async-start(), calls=%async_computation.2 | async-start | bytes 2359296 | tf_op jit(solution)/shard_map/psum | solution.py:58
  7.3 18.3 %copy-start.1 = (bf16[1024,1024]{1,0:T(8,128)(2,1)S(1)}, bf16[1024,1024]{1,0:T(8,128)(2,1)}, u32[]{:S(2)}) copy-start(bf16[1024,1024]{1,0:T(8,128)(2,1)} %param.13) | copy-start | bytes 6291460
  26.6 197.7 %reduce-scatter.3.cloned.1.call-start = ((), (), s32[]{:S(2)}) async-start(), calls=%async_computation.1 | async-start | bytes 1114112 | tf_op jit(solution)/shard_map/reduce_scatter | solution.py:102
  125.9 0.8 copy-start.2
Sparse Core Ops, SparseCore 0:
  26.7 96.7 all-reduce.3
  169.7 54.6 reduce-scatter.2
where the time goes:
time: 267 us
  blocking collectives  117 us (44%)
  waiting for transfers between devices  84 us (31%)
  matrix products  38 us (14%)
  between operations  14.9 us (6%)
  other arithmetic  9.5 us (4%)
  local copies, waits for them, and re-layouts  3.18 us (1%)
    psum x1, waiting for transfers between devices, on_device(): lax.psum((part_query, part_key, part_value, squares), 'gx')  61.3 us
    psum x1, blocking collectives, on_device(): lax.psum((part_query, part_key, part_value, squares), 'gx')  35.1 us
    pmax x1, blocking collectives, on_device(): score_peak = lax.pmax(jnp.maximum(block_peak, own_score), 'gx')  30.8 us
    unnamed x1, blocking collectives  30.1 us
    reduce_scatter x1, waiting for transfers between devices, on_device(): lax.psum_scatter(scaled_mix, 'gx', scatter_dimension=1, tiled=True)  22.6 us
    all_gather x1, blocking collectives, on_device(): lax.all_gather(head_out, 'gx', axis=1, tiled=True)  21 us
    dot_general x1, matrix products, on_device(): part_query = jnp.dot(scaled, w_query, preferred_element_type=jnp.float32)  16.5 us
    dot_general x1, matrix products, on_device(): jnp.dot(lax.all_gather(head_out, 'gx', axis=1, tiled=True), w_out, prefer...  13.4 us
  transfers between devices with their start and end apart: 2, of which 2 were waited for; matrix products, arithmetic and copies ran while one was open for 1% of the time, Pallas kernels for 0%

commit v1 on v0

v1 whole, which is shorter than its diff:
```python
import functools
import math

import jax
import jax.numpy as jnp
from jax import lax
from jax.experimental import pallas as pl
from jax.experimental.pallas import tpu as pltpu
from jax.sharding import PartitionSpec as P

HD = 128
EPS = 1e-05
BASE = 500000.0
SLOTS = 4
F32 = jnp.float32
BF16 = jnp.bfloat16


def kernel(
    n, hidden, gain, cos_ref, sin_ref, limit, wq, wk, wv, wo, ck, cv,
    out, new,
    wbuf, kvbuf, wobuf, ckb, cvb, kvp, part, sibr, dirr, qg, mixb, sibm, mixs, stats, mixr, statr,
    hacc, hg, acc,
    wsem, kvsem, wosem, csem, s1s, s1r, d1s, d1r, g1s, g1r, r1s, r1r, s2s, s2r, d2s, d2r, t2s, t2r,
    g2s, g2r, r2s, r2r,
):
    rows, depth = hidden.shape
    width = wbuf.shape[2]
    local = width // HD
    kv = ck.shape[1] // HD
    group = n * local // kv
    chips = n // 2
    per_kv = group // local
    chips_kv = per_kv // 2
    kv_devs = n // (2 * kv)
    spots = ck.shape[0] // rows
    me = lax.axis_index("gx")
    core = lax.rem(me, 2)
    chip = me // 2
    other = 1 - core
    sibling = 2 * chip + other

    def turn(index):
        return lax.rem(index + 2 * chips, chips)

    def remote(src, dst, send, recv, target):
        return pltpu.make_async_remote_copy(
            src_ref=src, dst_ref=dst, send_sem=send, recv_sem=recv,
            device_id={"gx": target}, device_id_type=pl.DeviceIdType.MESH,
        )

    def each_other(body):
        def step(u, carry):
            body(u)
            return carry
        lax.fori_loop(1, chips, step, 0)

    barrier = pltpu.get_barrier_semaphore()
    pl.semaphore_signal(barrier, inc=1, device_id={"gx": sibling}, device_id_type=pl.DeviceIdType.MESH)
    each_other(lambda u: pl.semaphore_signal(
        barrier, inc=1, device_id={"gx": 2 * turn(chip + u) + core}, device_id_type=pl.DeviceIdType.MESH))

    def load_w(t, second):
        c = turn(chip + 1 + t)
        d = 2 * c + (core if second else other)
        slot = lax.rem(2 * t + second, SLOTS)
        return pltpu.make_async_copy(
            wq.at[:, pl.ds(pl.multiple_of(d * width, HD), width)], wbuf.at[slot], wsem.at[slot])

    copy_k = pltpu.make_async_copy(wk, kvbuf.at[0], kvsem.at[0])
    copy_v = pltpu.make_async_copy(wv, kvbuf.at[1], kvsem.at[1])
    copy_k.start()
    copy_v.start()
    for t in range(SLOTS // 2):
        load_w(t, 0).start()
        load_w(t, 1).start()

    wide = hidden[...].astype(F32)
    squares = jnp.broadcast_to(jnp.sum(wide * wide, axis=1, keepdims=True), (rows, HD))
    scaled = (wide * gain[...].astype(F32)).astype(BF16)
    kv_width = kv * HD
    copy_k.wait()
    kvp[:, :kv_width] = jnp.dot(scaled, kvbuf[0], preferred_element_type=F32)
    copy_v.wait()
    kvp[:, kv_width:] = jnp.dot(scaled, kvbuf[1], preferred_element_type=F32)

    pl.semaphore_wait(barrier, chips)

    def sib1(c):
        return remote(part.at[2 * c + other], sibr.at[c], s1s.at[c], s1r.at[c], sibling)

    def dir1(c):
        return remote(part.at[2 * c + core], dirr.at[chip], d1s.at[c], d1r.at[chip], 2 * c + core)

    def dir1_in(c):
        return remote(part.at[me], dirr.at[c], d1s.at[c], d1r.at[c], 2 * c + core)

    def finish1(c):
        sib1(c).wait_recv()
        d = 2 * c + core
        part[d] = part[d] + sibr[c]

    def project(t, carry):
        c = turn(chip + 1 + t)
        for second in range(2):
            d = 2 * c + (core if second else other)
            slot = lax.rem(2 * t + second, SLOTS)
            load_w(t, second).wait()
            part[d, :, :width] = jnp.dot(scaled, wbuf[slot], preferred_element_type=F32)
            start = pl.multiple_of((d // kv_devs) * HD, HD)
            part[d, :, width:width + HD] = kvp[:, pl.ds(start, HD)]
            part[d, :, width + HD:] = squares

            @pl.when(t + SLOTS // 2 < chips)
            def _():
                load_w(t + SLOTS // 2, second).start()

            if not second:
                sib1(c).start()

        @pl.when(t > 0)
        def _():
            before = turn(chip + t)
            finish1(before)
            dir1(before).start()

        return carry

    lax.fori_loop(0, chips, project, 0)

    copy_ck = pltpu.make_async_copy(ck, ckb, csem.at[0])
    copy_cv = pltpu.make_async_copy(cv, cvb, csem.at[1])
    copy_ck.start()
    copy_cv.start()

    def load_wo(d):
        return pltpu.make_async_copy(
            wo.at[pl.ds(pl.multiple_of(d * width, HD), width), :], wobuf.at[d], wosem.at[d])

    def start_wo(i, carry):
        c = turn(chip - i)
        load_wo(2 * c + core).start()
        load_wo(2 * c + other).start()
        return carry

    lax.fori_loop(0, chips, start_wo, 0)

    finish1(chip)

    def gather1(u):
        c = turn(chip - u)
        dir1_in(c).wait_recv()
        part[me] = part[me] + dirr[c]

    each_other(gather1)

    inv = lax.rsqrt(part[me, :, width + HD:] / (depth * n) + EPS)
    cos_table, sin_table = cos_ref[...], sin_ref[...]
    for j in range(local):
        x = part[me, :, j * HD:(j + 1) * HD] * inv
        qg[me, :, j * HD:(j + 1) * HD] = (x * cos_table + pltpu.roll(x, HD // 2, 1) * sin_table).astype(BF16)
    is_key = (me // kv_devs < kv).astype(F32)
    x = part[me, :, width:width + HD] * inv
    cos_key = cos_table * is_key + (1.0 - is_key)
    qg[me, :, width:] = (x * cos_key + pltpu.roll(x, HD // 2, 1) * (sin_table * is_key)).astype(BF16)

    def out1(c):
        return remote(qg.at[me], qg.at[me], g1s.at[c], g1r.at[chip], 2 * c + core)

    def in1(c):
        return remote(qg.at[2 * c + core], qg.at[2 * c + core], g1s.at[c], g1r.at[c], 2 * c + core)

    def rel1(c):
        return remote(qg.at[2 * c + core], qg.at[2 * c + core], r1s.at[c], r1r.at[c], sibling)

    def rel1_in(c):
        return remote(qg.at[2 * c + other], qg.at[2 * c + other], r1s.at[c], r1r.at[c], sibling)

    rel1(chip).start()
    each_other(lambda u: out1(turn(chip + u)).start())

    def chips_of(k, body):
        def step(i, carry):
            body(k * chips_kv + i)
            return carry
        lax.fori_loop(0, chips_kv, step, 0)

    def relay1(k):
        def one(c):
            @pl.when(c != chip)
            def _():
                in1(c).wait_recv()
                rel1(c).start()
        chips_of(k, one)

    column = lax.broadcasted_iota(jnp.int32, (group * rows, rows * spots), 1)
    row = lax.broadcasted_iota(jnp.int32, (group * rows, rows * spots), 0)
    valid = (lax.rem(row, rows) == column // spots) & (limit[...] > me * spots)
    lane = lax.broadcasted_iota(jnp.int32, (rows, HD), 1)
    half = HD // 2

    def sib2(c):
        return remote(mixb.at[2 * c + other], sibm.at[c], s2s.at[c], s2r.at[c], sibling)

    def dir2(c, slot):
        return remote(mixs.at[c], mixr.at[slot], d2s.at[c], d2r.at[slot], 2 * c + core)

    def dir2_stat(c, slot):
        return remote(stats.at[c], statr.at[slot], t2s.at[c], t2r.at[slot], 2 * c + core)

    def finish2(k):
        def one(c):
            sib2(c).wait_recv()
            d = 2 * c + core
            first, second = mixb[d, :, width:], sibm[c, :, width:]
            top = jnp.maximum(first, second)
            e_first, e_second = jnp.exp(first - top), jnp.exp(second - top)
            total = pltpu.roll(first, half, 1) * e_first + pltpu.roll(second, half, 1) * e_second
            stats[c] = jnp.where(lane < half, top, pltpu.roll(total, half, 1))
            for j in range(local):
                at = slice(j * HD, (j + 1) * HD)
                mixs[c, :, at] = (
                    e_first[:, j:j + 1] * mixb[d, :, at] + e_second[:, j:j + 1] * sibm[c, :, at]
                ).astype(BF16)

            @pl.when(c != chip)
            def _():
                dir2(c, chip).start()
                dir2_stat(c, chip).start()
        chips_of(k, one)

    first_kv = chip // chips_kv

    def kv_at(t):
        return lax.rem(first_kv - t + 2 * kv, kv)

    relay1(first_kv)
    copy_ck.wait()
    copy_cv.wait()

    def attend(t, carry):
        k = kv_at(t)

        @pl.when(t + 1 < kv)
        def _():
            relay1(kv_at(t + 1))

        chips_of(k, lambda c: rel1_in(c).wait_recv())
        query = jnp.concatenate(
            [qg[k * per_kv + h // local, :, (h % local) * HD:(h % local + 1) * HD] for h in range(group)], axis=0)
        at = pl.ds(pl.multiple_of(k * HD, HD), HD)
        scores = lax.dot_general(
            query, ckb[:, at], (((1,), (1,)), ((), ())), preferred_element_type=F32) * (HD ** -0.5)
        scores = jnp.where(valid, scores, -1e30)
        peak = jnp.max(scores, axis=1, keepdims=True)
        weights = jnp.where(valid, jnp.exp(scores - peak), 0.0)
        total = jnp.sum(weights, axis=1, keepdims=True)
        mix = jnp.dot(weights.astype(BF16), cvb[:, at], preferred_element_type=F32)
        for i in range(per_kv):
            d = k * per_kv + i
            stat = jnp.zeros((rows, HD), F32)
            for j in range(local):
                h = i * local + j
                here = slice(h * rows, (h + 1) * rows)
                mixb[d, :, j * HD:(j + 1) * HD] = mix[here]
                stat = jnp.where(lane == j, peak[here], stat)
                stat = jnp.where(lane == half + j, total[here], stat)
            mixb[d, :, width:] = stat
        chips_of(k, lambda c: sib2(c).start())

        @pl.when(t > 0)
        def _():
            finish2(kv_at(t - 1))

        return carry

    lax.fori_loop(0, kv, attend, 0)
    finish2(kv_at(kv - 1))

    for i in range(kv):
        new[0, :, i * HD:(i + 1) * HD] = qg[i * kv_devs, :, width:]
        new[1, :, i * HD:(i + 1) * HD] = qg[(kv + i) * kv_devs, :, width:]

    my_kv = me * local // group
    own_key = qg[my_kv * kv_devs, :, width:].astype(F32)
    own_value = qg[(kv + my_kv) * kv_devs, :, width:].astype(F32)
    own = jnp.zeros((rows, HD), F32)
    for j in range(local):
        score = jnp.sum(qg[me, :, j * HD:(j + 1) * HD].astype(F32) * own_key, axis=1, keepdims=True)
        own = jnp.where(lane == j, score * (HD ** -0.5), own)

    statr[chip] = stats[chip]
    mixr[chip] = mixs[chip]

    def peaks(u, top):
        c = turn(chip - u)
        dir2_stat(c, c).wait_recv()
        return jnp.maximum(top, statr[c])

    top = lax.fori_loop(1, chips, peaks, jnp.maximum(own, stats[chip]))
    own_weight = jnp.exp(own - top)
    for j in range(local):
        hacc[:, j * HD:(j + 1) * HD] = own_weight[:, j:j + 1] * own_value

    def add(c, total):
        stat = statr[c]
        scale = jnp.exp(stat - top)
        for j in range(local):
            at = slice(j * HD, (j + 1) * HD)
            hacc[:, at] = hacc[:, at] + scale[:, j:j + 1] * mixr[c, :, at].astype(F32)
        return total + scale * pltpu.roll(stat, half, 1)

    def add_other(u, total):
        c = turn(chip - u)
        dir2(c, c).wait_recv()
        return add(c, total)

    total = lax.fori_loop(1, chips, add_other, add(chip, own_weight))
    for j in range(local):
        at = slice(j * HD, (j + 1) * HD)
        hg[me, :, at] = (hacc[:, at] / total[:, j:j + 1]).astype(BF16)

    def out2(c):
        return remote(hg.at[me], hg.at[me], g2s.at[c], g2r.at[chip], 2 * c + core)

    def in2(c):
        return remote(hg.at[2 * c + core], hg.at[2 * c + core], g2s.at[c], g2r.at[c], 2 * c + core)

    def rel2(c):
        return remote(hg.at[2 * c + core], hg.at[2 * c + core], r2s.at[c], r2r.at[c], sibling)

    def rel2_in(c):
        return remote(hg.at[2 * c + other], hg.at[2 * c + other], r2s.at[c], r2r.at[c], sibling)

    rel2(chip).start()
    each_other(lambda u: out2(turn(chip + u)).start())

    def product(d):
        load_wo(d).wait()
        acc[...] = acc[...] + jnp.dot(hg[d], wobuf[d], preferred_element_type=F32)

    acc[...] = jnp.zeros_like(acc)
    product(me)

    def project_out(u):
        c = turn(chip - u)
        in2(c).wait_recv()
        rel2(c).start()
        before = turn(chip - u + 1)
        rel2_in(before).wait_recv()
        product(2 * before + other)
        product(2 * c + core)

    each_other(project_out)
    last = turn(chip + 1)
    rel2_in(last).wait_recv()
    product(2 * last + other)
    out[...] = acc[...].astype(BF16)

    def drain(c, carry):
        sib1(c).wait_send()
        rel1(c).wait_send()
        sib2(c).wait_send()
        rel2(c).wait_send()

        @pl.when(c != chip)
        def _():
            dir1(c).wait_send()
            out1(c).wait_send()
            dir2(c, chip).wait_send()
            dir2_stat(c, chip).wait_send()
            out2(c).wait_send()

        return carry

    lax.fori_loop(0, chips, drain, 0)


def on_device(hidden, norm_gain, w_query, w_key, w_value, w_out, cache_keys, cache_values, lengths):
    n = lax.axis_size("gx")
    rows, depth = hidden.shape
    spots, kv_width = cache_keys.shape[1:]
    width = w_query.shape[1] // n
    out_width = w_out.shape[1]
    chips = n // 2
    half = HD // 2
    frequency = jnp.exp(jnp.arange(half, dtype=F32) * (-2.0 * math.log(BASE) / HD))
    angles = lengths.astype(F32)[:, None] * frequency[None, :]
    cos_half, sin_half = jnp.cos(angles), jnp.sin(angles)
    cos_table = jnp.concatenate([cos_half, cos_half], axis=1)
    sin_table = jnp.concatenate([-sin_half, sin_half], axis=1)
    limit = (lengths[:, None] - jnp.arange(spots, dtype=jnp.int32)[None, :]).reshape(1, rows * spots)
    vmem = pl.BlockSpec(memory_space=pltpu.VMEM)
    hbm = pl.BlockSpec(memory_space=pl.ANY)
    dma = pltpu.SemaphoreType.DMA
    return pl.pallas_call(
        functools.partial(kernel, n),
        out_shape=(
            jax.ShapeDtypeStruct((rows, out_width), BF16),
            jax.ShapeDtypeStruct((2, rows, kv_width), BF16),
        ),
        in_specs=[vmem] * 5 + [hbm] * 6,
        out_specs=(vmem, vmem),
        scratch_shapes=[
            pltpu.VMEM((SLOTS, depth, width), BF16),
            pltpu.VMEM((2, depth, kv_width), BF16),
            pltpu.VMEM((n, width, out_width), BF16),
            pltpu.VMEM((rows * spots, kv_width), BF16),
            pltpu.VMEM((rows * spots, kv_width), BF16),
            pltpu.VMEM((rows, 2 * kv_width), F32),
            pltpu.VMEM((n, rows, width + 2 * HD), F32),
            pltpu.VMEM((chips, rows, width + 2 * HD), F32),
            pltpu.VMEM((chips, rows, width + 2 * HD), F32),
            pltpu.VMEM((n, rows, width + HD), BF16),
            pltpu.VMEM((n, rows, width + HD), F32),
            pltpu.VMEM((chips, rows, width + HD), F32),
            pltpu.VMEM((chips, rows, width), BF16),
            pltpu.VMEM((chips, rows, HD), F32),
            pltpu.VMEM((chips, rows, width), BF16),
            pltpu.VMEM((chips, rows, HD), F32),
            pltpu.VMEM((rows, width), F32),
            pltpu.VMEM((n, rows, width), BF16),
            pltpu.VMEM((rows, out_width), F32),
            dma((SLOTS,)), dma((2,)), dma((n,)), dma((2,)),
        ] + [dma((chips,)) for _ in range(18)],
        compiler_params=pltpu.CompilerParams(
            collective_id=0, has_side_effects=True, vmem_limit_bytes=60 * 1024 * 1024),
        cost_estimate=pl.CostEstimate(
            flops=4 * rows * depth * n * width, bytes_accessed=4 * depth * n * width, transcendentals=0),
    )(
        hidden, norm_gain.reshape(1, depth), cos_table, sin_table, limit, w_query, w_key, w_value, w_out,
        cache_keys.reshape(rows * spots, kv_width), cache_values.reshape(rows * spots, kv_width),
    )


def solution(mesh):
    return jax.shard_map(
        on_device,
        mesh=mesh,
        in_specs=(
            P("grp", "gx"),
            P("gx"),
            P("gx", None),
            P("gx", None),
            P("gx", None),
            P(None, "gx"),
            P("grp", "gx", None),
            P("grp", "gx", None),
            P("grp"),
        ),
        out_specs=(P("grp", "gx"), P(None, "grp", None)),
        check_vma=False,
    )
```

time: 267 us -> 67.1 us (0.25)
  blocking collectives: 117 us -> 0 us
  waiting for transfers between devices: 84 us -> 0 us
  Pallas kernels: 0 us -> 59.1 us
  matrix products: 38 us -> 0 us
  between operations: 14.9 us -> 0.64 us
  other arithmetic: 9.5 us -> 2.19 us
    psum x1 -> x0, waiting for transfers between devices: 61.3 us -> none  [on_device(): lax.psum((part_query, part_key, part_value, squares), 'gx')]
    pallas_call x0 -> x1, Pallas kernels: none -> 59.1 us  [on_device(): pl.pallas_call(functools.partial(kernel, n), out_shape=(jax.ShapeDtypeStr...]
    dot_general x7 -> x0, matrix products: 38 us -> none  [the longest x1 16.5 us: on_device(): part_query = jnp.dot(scaled, w_query, preferred_element_type=jnp.float32)]
    psum x1 -> x0, blocking collectives: 35.1 us -> none  [on_device(): lax.psum((part_query, part_key, part_value, squares), 'gx')]
    pmax x1 -> x0, blocking collectives: 30.8 us -> none  [on_device(): score_peak = lax.pmax(jnp.maximum(block_peak, own_score), 'gx')]
    unnamed x1 -> x0, blocking collectives: 30.1 us -> none
    reduce_scatter x1 -> x0, waiting for transfers between devices: 22.6 us -> none  [on_device(): lax.psum_scatter(scaled_mix, 'gx', scatter_dimension=1, tiled=True)]
    all_gather x1 -> x0, blocking collectives: 21 us -> none  [on_device(): lax.all_gather(head_out, 'gx', axis=1, tiled=True)]
  transfers between devices with their start and end apart: 2 -> 0, of which waited for: 2 -> 0; matrix products, arithmetic and copies ran while one was open for 1% -> 0% of each run, Pallas kernels for 0% -> 0%
where the time goes in v1:
time: 67.1 us; the launch traced here: 66.7 us
  Pallas kernels  59.1 us (88%)
  local copies, waits for them, and re-layouts  4.77 us (7%)
  other arithmetic  2.19 us (3%)
    pallas_call x1, Pallas kernels, on_device(): pl.pallas_call(functools.partial(kernel, n), out_shape=(jax.ShapeDtypeStr...  59.1 us
    unnamed x2, local copies, waits for them, and re-layouts  2.85 us

profile of v1, /device:TPU:0, one launch (start us, length us, event | category | flops | bytes accessed | tf_op | source)
XLA Modules:
  0.0 66.7 jit_solution(7265664820444707630)
XLA Ops:
  0.6 0.7 convert_element_type.3
  1.3 1.3 %reshape.43.gain = bf16[1,1024]{1,0:T(2,128)(2,1)} reshape(bf16[1024]{0:T(1024)(128)(2,1)} %param.10) | data formatting | bytes 4096 | tf_op jit(solution)/shard_map/reshape | solution.py:431
  2.6 0.7 %iota_subtract_fusion = s32[16,32]{1,0:T(8,128)S(1)} fusion(s32[16]{0:T(128)} %param.17), kind=kLoop, calls=%fused_computation.4 | loop fusion | flops 512 | bytes 2112 | tf_op jit(solution)/shard_map/sub | solution.py:392
  3.3 0.6 sub.26.limit
  4.0 0.1 fusion
  4.1 0.7 %pad_maximum_fusion = (f32[16,128]{1,0:T(8,128)}, f32[16,128]{1,0:T(8,128)}) fusion(f32[16,64]{1,0:T(8,128)S(1)} %get-tuple-element.4, f32[16,64]{1,0:T(8,128)S(1)} %get-tuple-element.3, f32[16,64]{1,0:T(8,128)S(1)} %get-tuple-element.2), kind=kLoop, calls=%fused_computation.2 | loop fusion | flops 4096 | bytes 28672 | tf_op jit(solution)/shard_map/concatenate | solution.py:390
  4.8 59.1 %shard_map.104 = (bf16[16,1024]{1,0:T(8,128)(2,1)}, bf16[2,16,1024]{2,1,0:T(8,128)(2,1)}) custom-call(bf16[16,1024]{1,0:T(8,128)(2,1)} %hidden.1, bf16[1,1024]{1,0:T(2,128)(2,1)} %reshape.43.gain, f32[16,128]{1,0:T(8,128)} %get-tuple-element.5.cos_ref, f32[16,128]{1,0:T(8,128)} %get-tuple-element.6.sin_ref, s32[1,512]{1,0:T(1,128)} %sub.26.limit, ...), custom_call_target="tpu_custom_call" | custom-call | flops 1073741824 | bytes 67108864 | tf_op jit(solution)/shard_map/pallas_call | solution.py:396
  63.8 1.4 %copy.13 = bf16[16,1024]{1,0:T(8,128)(2,1)} copy(bf16[16,1024]{1,0:T(8,128)(2,1)} %get-tuple-element.9) | data formatting | bytes 65536
  65.2 1.5 %copy.14 = bf16[2,16,1024]{2,1,0:T(8,128)(2,1)} copy(bf16[2,16,1024]{2,1,0:T(8,128)(2,1)} %get-tuple-element.10) | data formatting | bytes 131072
  (1 shorter events, 0.0 us)

commit v2 on v1

v2 whole, which is shorter than its diff:
```python
import functools
import math

import jax
import jax.numpy as jnp
from jax import lax
from jax.experimental import pallas as pl
from jax.experimental.pallas import tpu as pltpu
from jax.sharding import PartitionSpec as P

HD = 128
EPS = 1e-05
BASE = 500000.0
AHEAD = 8
F32 = jnp.float32
BF16 = jnp.bfloat16


def kernel(
    n, hidden, gain, lengths, wq, wk, wv, wo, ck, cv,
    out, new,
    wbuf, kvbuf, ckb, cvb, kvp, part, sibr, yr, zr, qg, mixb, sibm, ym, zm, hacc, hg, acc,
    wsem, kvsem, wosem, csem, s1s, s1r, y1s, y1r, z1s, z1r, gss, gsr, gys, gyr, gzs, gzr,
    s2s, s2r, y2s, y2r, z2s, z2r, hss, hsr, hys, hyr, hzs, hzr,
):
    rows, depth = hidden.shape
    width = wbuf.shape[2]
    local = width // HD
    kv = ck.shape[1] // HD
    group = n * local // kv
    chips = n // 2
    pairs = chips // 2
    per_kv = group // local
    chips_kv = per_kv // 2
    kv_devs = n // (2 * kv)
    spots = ck.shape[0] // rows
    half = HD // 2
    me = lax.axis_index("gx")
    core = lax.rem(me, 2)
    chip = me // 2
    side = lax.rem(chip, 2)
    pair = chip // 2
    other = 1 - core
    sibling = 2 * chip + other
    across = 2 * (2 * pair + 1 - side) + core

    def turn(index):
        return lax.rem(index + 2 * pairs, pairs)

    def near(p):
        return 2 * p + side

    def far(p):
        return 2 * p + 1 - side

    def along(p):
        return 2 * near(p) + core

    def remote(src, dst, send, recv, target):
        return pltpu.make_async_remote_copy(
            src_ref=src, dst_ref=dst, send_sem=send, recv_sem=recv,
            device_id={"gx": target}, device_id_type=pl.DeviceIdType.MESH,
        )

    def each_other(body):
        def step(u, carry):
            body(turn(pair - u))
            return carry
        lax.fori_loop(1, pairs, step, 0)

    barrier = pltpu.get_barrier_semaphore()

    def greet(target):
        pl.semaphore_signal(barrier, inc=1, device_id={"gx": target}, device_id_type=pl.DeviceIdType.MESH)

    greet(sibling)
    greet(across)
    each_other(lambda p: greet(along(p)))

    def block(t, second):
        c = 2 * turn(pair + 1 + t // 2) + lax.rem(side + 1 + t, 2)
        return c, 2 * c + (core if second else other)

    def load_w(t, second):
        d = block(t, second)[1]
        return pltpu.make_async_copy(
            wq.at[:, pl.ds(pl.multiple_of(d * width, HD), width)], wbuf.at[d], wsem.at[d])

    copy_k = pltpu.make_async_copy(wk, kvbuf.at[0], kvsem.at[0])
    copy_v = pltpu.make_async_copy(wv, kvbuf.at[1], kvsem.at[1])
    copy_k.start()
    copy_v.start()
    for t in range(AHEAD // 2):
        load_w(t, 0).start()
        load_w(t, 1).start()

    row_at = lax.broadcasted_iota(jnp.int32, (rows, HD), 0)
    lane = lax.broadcasted_iota(jnp.int32, (rows, HD), 1)
    owner_row = lax.broadcasted_iota(jnp.int32, (1, rows * spots), 1)
    by_row = jnp.zeros((rows, HD), jnp.int32)
    by_column = jnp.zeros((1, rows * spots), jnp.int32)
    for r in range(rows):
        size = lengths[r]
        by_row = jnp.where(row_at == r, size, by_row)
        by_column = jnp.where(owner_row // spots == r, size, by_column)
    limit = by_column - lax.rem(owner_row, spots)
    frequency = jnp.exp(lax.rem(lane, half).astype(F32) * (-2.0 * math.log(BASE) / HD))
    angles = by_row.astype(F32) * frequency
    cos_table = jnp.cos(angles)
    sin_table = jnp.sin(angles)
    sin_table = jnp.where(lane < half, -sin_table, sin_table)

    wide = hidden[...].astype(F32)
    squares = jnp.broadcast_to(jnp.sum(wide * wide, axis=1, keepdims=True), (rows, HD))
    scaled = (wide * gain[...].astype(F32)[None, :]).astype(BF16)
    kv_width = kv * HD
    copy_k.wait()
    kvp[:, :kv_width] = jnp.dot(scaled, kvbuf[0], preferred_element_type=F32)
    copy_v.wait()
    kvp[:, kv_width:] = jnp.dot(scaled, kvbuf[1], preferred_element_type=F32)

    pl.semaphore_wait(barrier, pairs + 1)

    def sib1(c):
        return remote(part.at[2 * c + other], sibr.at[c], s1s.at[c], s1r.at[c], sibling)

    def y1(p):
        return remote(part.at[2 * far(p) + core], yr.at[p], y1s.at[p], y1r.at[p], across)

    def z1(p):
        return remote(part.at[along(p)], zr.at[pair], z1s.at[p], z1r.at[pair], along(p))

    def z1_in(p):
        return remote(part.at[me], zr.at[p], z1s.at[p], z1r.at[p], along(p))

    def finish1_far(p):
        c = far(p)
        sib1(c).wait_recv()
        part[2 * c + core] = part[2 * c + core] + sibr[c]
        y1(p).start()

    def finish1_near(p):
        c = near(p)
        sib1(c).wait_recv()
        y1(p).wait_recv()
        part[2 * c + core] = part[2 * c + core] + sibr[c] + yr[p]

    def project_side(i, is_near):
        t = 2 * i + is_near
        for second in range(2):
            c, d = block(t, second)
            load_w(t, second).wait()
            part[d, :, :width] = jnp.dot(scaled, wbuf[d], preferred_element_type=F32)
            start = pl.multiple_of((d // kv_devs) * HD, HD)
            part[d, :, width:width + HD] = kvp[:, pl.ds(start, HD)]
            part[d, :, width + HD:] = squares

            @pl.when(t + AHEAD // 2 < chips)
            def _():
                load_w(t + AHEAD // 2, second).start()

            if not second:
                sib1(c).start()

    def project(i, carry):
        project_side(i, 0)

        @pl.when(i > 0)
        def _():
            before = turn(pair + i)
            finish1_near(before)
            z1(before).start()

        project_side(i, 1)
        finish1_far(turn(pair + 1 + i))
        return carry

    lax.fori_loop(0, pairs, project, 0)

    copy_ck = pltpu.make_async_copy(ck, ckb, csem.at[0])
    copy_cv = pltpu.make_async_copy(cv, cvb, csem.at[1])
    copy_ck.start()
    copy_cv.start()

    def load_wo(d):
        return pltpu.make_async_copy(
            wo.at[pl.ds(pl.multiple_of(d * width, HD), width), :], wbuf.at[d], wosem.at[d])

    def start_wo(i, carry):
        p = turn(pair - i)
        for c in (near(p), far(p)):
            load_wo(2 * c + core).start()
            load_wo(2 * c + other).start()
        return carry

    lax.fori_loop(0, pairs, start_wo, 0)

    finish1_near(pair)

    def gather1(p):
        z1_in(p).wait_recv()
        part[me] = part[me] + zr[p]

    each_other(gather1)

    inv = lax.rsqrt(part[me, :, width + HD:] / (depth * n) + EPS)
    for j in range(local):
        x = part[me, :, j * HD:(j + 1) * HD] * inv
        qg[me, :, j * HD:(j + 1) * HD] = (x * cos_table + pltpu.roll(x, half, 1) * sin_table).astype(BF16)
    is_key = (me // kv_devs < kv).astype(F32)
    x = part[me, :, width:width + HD] * inv
    cos_key = cos_table * is_key + (1.0 - is_key)
    qg[me, :, width:] = (x * cos_key + pltpu.roll(x, half, 1) * (sin_table * is_key)).astype(BF16)

    class Spread:
        def __init__(self, ref, ss, sr, ys, yr_, zs, zr_):
            self.ref, self.sems = ref, (ss, sr, ys, yr_, zs, zr_)

        def to_sibling(self, c):
            ss, sr = self.sems[:2]
            at = self.ref.at[2 * c + core]
            return remote(at, at, ss.at[c], sr.at[c], sibling)

        def from_sibling(self, c):
            ss, sr = self.sems[:2]
            at = self.ref.at[2 * c + other]
            return remote(at, at, ss.at[c], sr.at[c], sibling)

        def to_across(self, p):
            ys, yr_ = self.sems[2:4]
            at = self.ref.at[along(p)]
            return remote(at, at, ys.at[p], yr_.at[p], across)

        def from_across(self, p):
            ys, yr_ = self.sems[2:4]
            at = self.ref.at[2 * far(p) + core]
            return remote(at, at, ys.at[p], yr_.at[p], across)

        def to_along(self, p):
            zs, zr_ = self.sems[4:]
            at = self.ref.at[me]
            return remote(at, at, zs.at[p], zr_.at[pair], along(p))

        def from_along(self, p):
            zs, zr_ = self.sems[4:]
            at = self.ref.at[along(p)]
            return remote(at, at, zs.at[p], zr_.at[p], along(p))

        def begin(self):
            def send(u, carry):
                self.to_along(turn(pair + u)).start()
                return carry
            lax.fori_loop(1, pairs, send, 0)
            self.to_across(pair).start()
            self.to_sibling(chip).start()

        def relay_near(self, p):
            self.from_along(p).wait_recv()
            self.to_across(p).start()
            self.to_sibling(near(p)).start()

        def relay_far(self, p):
            self.from_across(p).wait_recv()
            self.to_sibling(far(p)).start()

    spread1 = Spread(qg, gss, gsr, gys, gyr, gzs, gzr)
    spread1.begin()

    column = lax.broadcasted_iota(jnp.int32, (group * rows, rows * spots), 1)
    row = lax.broadcasted_iota(jnp.int32, (group * rows, rows * spots), 0)
    valid = (lax.rem(row, rows) == column // spots) & (limit > me * spots)

    def sib2(c):
        return remote(mixb.at[2 * c + other], sibm.at[c], s2s.at[c], s2r.at[c], sibling)

    def y2(p):
        return remote(mixb.at[2 * far(p) + core], ym.at[p], y2s.at[p], y2r.at[p], across)

    def z2(p):
        return remote(mixb.at[along(p)], zm.at[pair], z2s.at[p], z2r.at[pair], along(p))

    def z2_in(p):
        return remote(mixb.at[me], zm.at[p], z2s.at[p], z2r.at[p], along(p))

    def merge(d, from_ref, index):
        first, second = mixb[d, :, width:], from_ref[index, :, width:]
        top = jnp.maximum(first, second)
        e_first, e_second = jnp.exp(first - top), jnp.exp(second - top)
        total = pltpu.roll(first, half, 1) * e_first + pltpu.roll(second, half, 1) * e_second
        mixb[d, :, width:] = jnp.where(lane < half, top, pltpu.roll(total, half, 1))
        for j in range(local):
            at = slice(j * HD, (j + 1) * HD)
            mixb[d, :, at] = e_first[:, j:j + 1] * mixb[d, :, at] + e_second[:, j:j + 1] * from_ref[index, :, at]

    def finish2_far(p):
        c = far(p)
        sib2(c).wait_recv()
        merge(2 * c + core, sibm, c)
        y2(p).start()

    def finish2_near(p):
        c = near(p)
        sib2(c).wait_recv()
        merge(2 * c + core, sibm, c)
        y2(p).wait_recv()
        merge(2 * c + core, ym, p)

        @pl.when(p != pair)
        def _():
            z2(p).start()

    def attend(k):
        query = jnp.concatenate(
            [qg[k * per_kv + h // local, :, (h % local) * HD:(h % local + 1) * HD] for h in range(group)], axis=0)
        at = pl.ds(pl.multiple_of(k * HD, HD), HD)
        scores = lax.dot_general(
            query, ckb[:, at], (((1,), (1,)), ((), ())), preferred_element_type=F32) * (HD ** -0.5)
        scores = jnp.where(valid, scores, -1e30)
        peak = jnp.max(scores, axis=1, keepdims=True)
        weights = jnp.where(valid, jnp.exp(scores - peak), 0.0)
        total = jnp.sum(weights, axis=1, keepdims=True)
        mix = jnp.dot(weights.astype(BF16), cvb[:, at], preferred_element_type=F32)
        for i in range(per_kv):
            d = k * per_kv + i
            stat = jnp.zeros((rows, HD), F32)
            for j in range(local):
                h = i * local + j
                here = slice(h * rows, (h + 1) * rows)
                mixb[d, :, j * HD:(j + 1) * HD] = mix[here]
                stat = jnp.where(lane == j, peak[here], stat)
                stat = jnp.where(lane == half + j, total[here], stat)
            mixb[d, :, width:] = stat

        def send(i, carry):
            sib2(k * chips_kv + i).start()
            return carry

        lax.fori_loop(0, chips_kv, send, 0)

    if chips_kv == 1:
        copy_ck.wait()
        copy_cv.wait()
        spread1.from_sibling(chip).wait_recv()
        attend(chip)
        spread1.relay_far(pair)
        spread1.relay_near(turn(pair - 1))
        spread1.from_sibling(far(pair)).wait_recv()
        attend(far(pair))

        def of_pair(u, carry):
            p = turn(pair - u)
            spread1.relay_far(p)

            @pl.when(u + 1 < pairs)
            def _():
                spread1.relay_near(turn(pair - u - 1))

            spread1.from_sibling(far(p)).wait_recv()
            attend(far(p))
            finish2_far(turn(p + 1))
            spread1.from_sibling(near(p)).wait_recv()
            attend(near(p))

            @pl.when(u > 1)
            def _():
                finish2_near(turn(p + 1))

            return carry

        lax.fori_loop(1, pairs, of_pair, 0)
        last = turn(pair + 1)
        finish2_far(last)
        finish2_near(last)
        finish2_near(pair)
    else:
        each_other(spread1.relay_near)
        spread1.relay_far(pair)
        each_other(spread1.relay_far)
        copy_ck.wait()
        copy_cv.wait()

        def wait_chip(c, carry):
            spread1.from_sibling(c).wait_recv()
            return carry

        lax.fori_loop(0, chips, wait_chip, 0)

        def of_kv(k, carry):
            attend(k)

            def finish_far(i, inner):
                finish2_far(k * chips_kv // 2 + i)
                return inner

            def finish_near(i, inner):
                finish2_near(k * chips_kv // 2 + i)
                return inner

            lax.fori_loop(0, chips_kv // 2, finish_far, 0)
            lax.fori_loop(0, chips_kv // 2, finish_near, 0)
            return carry

        lax.fori_loop(0, kv, of_kv, 0)

    for i in range(kv):
        new[0, :, i * HD:(i + 1) * HD] = qg[i * kv_devs, :, width:]
        new[1, :, i * HD:(i + 1) * HD] = qg[(kv + i) * kv_devs, :, width:]

    my_kv = me * local // group
    own_key = qg[my_kv * kv_devs, :, width:].astype(F32)
    own_value = qg[(kv + my_kv) * kv_devs, :, width:].astype(F32)
    own = jnp.zeros((rows, HD), F32)
    for j in range(local):
        score = jnp.sum(qg[me, :, j * HD:(j + 1) * HD].astype(F32) * own_key, axis=1, keepdims=True)
        own = jnp.where(lane == j, score * (HD ** -0.5), own)

    def peaks(u, top):
        p = turn(pair - u)
        z2_in(p).wait_recv()
        return jnp.maximum(top, zm[p, :, width:])

    my_stat = mixb[me, :, width:]
    top = lax.fori_loop(1, pairs, peaks, jnp.maximum(own, my_stat))
    own_weight = jnp.exp(own - top)
    scale = jnp.exp(my_stat - top)
    for j in range(local):
        at = slice(j * HD, (j + 1) * HD)
        hacc[:, at] = own_weight[:, j:j + 1] * own_value + scale[:, j:j + 1] * mixb[me, :, at]

    def add(u, total):
        p = turn(pair - u)
        stat = zm[p, :, width:]
        scale = jnp.exp(stat - top)
        for j in range(local):
            at = slice(j * HD, (j + 1) * HD)
            hacc[:, at] = hacc[:, at] + scale[:, j:j + 1] * zm[p, :, at]
        return total + scale * pltpu.roll(stat, half, 1)

    total = lax.fori_loop(1, pairs, add, own_weight + scale * pltpu.roll(my_stat, half, 1))
    for j in range(local):
        at = slice(j * HD, (j + 1) * HD)
        hg[me, :, at] = (hacc[:, at] / total[:, j:j + 1]).astype(BF16)

    spread2 = Spread(hg, hss, hsr, hys, hyr, hzs, hzr)
    spread2.begin()

    def product(d):
        load_wo(d).wait()
        acc[...] = acc[...] + jnp.dot(hg[d], wbuf[d], preferred_element_type=F32)

    acc[...] = jnp.zeros_like(acc)
    product(me)
    spread2.relay_far(pair)
    spread2.from_sibling(chip).wait_recv()
    product(sibling)

    def project_out(p):
        spread2.relay_near(p)
        before = turn(p + 1)
        product(2 * far(before) + core)
        spread2.from_sibling(far(before)).wait_recv()
        product(2 * far(before) + other)
        spread2.relay_far(p)
        product(along(p))
        spread2.from_sibling(near(p)).wait_recv()
        product(2 * near(p) + other)

    each_other(project_out)
    last = turn(pair + 1)
    product(2 * far(last) + core)
    spread2.from_sibling(far(last)).wait_recv()
    product(2 * far(last) + other)
    out[...] = acc[...].astype(BF16)

    def drain_chip(c, carry):
        sib1(c).wait_send()
        sib2(c).wait_send()
        spread1.to_sibling(c).wait_send()
        spread2.to_sibling(c).wait_send()
        return carry

    def drain_pair(p, carry):
        y1(p).wait_send()
        y2(p).wait_send()
        spread1.to_across(p).wait_send()
        spread2.to_across(p).wait_send()
        return carry

    def drain_along(p):
        z1(p).wait_send()
        z2(p).wait_send()
        spread1.to_along(p).wait_send()
        spread2.to_along(p).wait_send()

    lax.fori_loop(0, chips, drain_chip, 0)
    lax.fori_loop(0, pairs, drain_pair, 0)
    each_other(drain_along)


def on_device(hidden, norm_gain, w_query, w_key, w_value, w_out, cache_keys, cache_values, lengths):
    n = lax.axis_size("gx")
    rows, depth = hidden.shape
    spots, kv_width = cache_keys.shape[1:]
    width = w_query.shape[1] // n
    out_width = w_out.shape[1]
    chips = n // 2
    pairs = chips // 2
    vmem = pl.BlockSpec(memory_space=pltpu.VMEM)
    hbm = pl.BlockSpec(memory_space=pl.ANY)
    dma = pltpu.SemaphoreType.DMA
    return pl.pallas_call(
        functools.partial(kernel, n),
        out_shape=(
            jax.ShapeDtypeStruct((rows, out_width), BF16),
            jax.ShapeDtypeStruct((2, rows, kv_width), BF16),
        ),
        in_specs=[vmem, vmem, pl.BlockSpec(memory_space=pltpu.SMEM)] + [hbm] * 6,
        out_specs=(vmem, vmem),
        scratch_shapes=[
            pltpu.VMEM((n, depth, width), BF16),
            pltpu.VMEM((2, depth, kv_width), BF16),
            pltpu.VMEM((rows * spots, kv_width), BF16),
            pltpu.VMEM((rows * spots, kv_width), BF16),
            pltpu.VMEM((rows, 2 * kv_width), F32),
            pltpu.VMEM((n, rows, width + 2 * HD), F32),
            pltpu.VMEM((chips, rows, width + 2 * HD), F32),
            pltpu.VMEM((pairs, rows, width + 2 * HD), F32),
            pltpu.VMEM((pairs, rows, width + 2 * HD), F32),
            pltpu.VMEM((n, rows, width + HD), BF16),
            pltpu.VMEM((n, rows, width + HD), F32),
            pltpu.VMEM((chips, rows, width + HD), F32),
            pltpu.VMEM((pairs, rows, width + HD), F32),
            pltpu.VMEM((pairs, rows, width + HD), F32),
            pltpu.VMEM((rows, width), F32),
            pltpu.VMEM((n, rows, width), BF16),
            pltpu.VMEM((rows, out_width), F32),
            dma((n,)), dma((2,)), dma((n,)), dma((2,)),
        ] + [dma((size,)) for size in (chips, chips, pairs, pairs, pairs, pairs) * 4],
        compiler_params=pltpu.CompilerParams(
            collective_id=0, has_side_effects=True, vmem_limit_bytes=60 * 1024 * 1024),
        cost_estimate=pl.CostEstimate(
            flops=4 * rows * depth * n * width, bytes_accessed=4 * depth * n * width, transcendentals=0),
    )(
        hidden, norm_gain, lengths, w_query, w_key, w_value, w_out,
        cache_keys.reshape(rows * spots, kv_width), cache_values.reshape(rows * spots, kv_width),
    )


def solution(mesh):
    return jax.shard_map(
        on_device,
        mesh=mesh,
        in_specs=(
            P("grp", "gx"),
            P("gx"),
            P("gx", None),
            P("gx", None),
            P("gx", None),
            P(None, "gx"),
            P("grp", "gx", None),
            P("grp", "gx", None),
            P("grp"),
        ),
        out_specs=(P("grp", "gx"), P(None, "grp", None)),
        check_vma=False,
    )
```

time: 67.1 us -> 78.4 us (1.17)
  Pallas kernels: 59.1 us -> 74.6 us
  other arithmetic: 2.19 us -> 0 us
  local copies, waits for them, and re-layouts: 4.77 us -> 2.85 us
    pallas_call x1, Pallas kernels: 59.1 us -> 74.6 us  [on_device(): pl.pallas_call(functools.partial(kernel, n), out_shape=(jax.ShapeDtypeStr...]
    reshape x1 -> x0, local copies, waits for them, and re-layouts: 1.28 us -> none  [on_device(): norm_gain.reshape(1, depth)]
where the time goes in v2:
time: 78.4 us; the launch traced here: 78.1 us
  Pallas kernels  74.6 us (95%)
  local copies, waits for them, and re-layouts  2.85 us (4%)
    pallas_call x1, Pallas kernels, on_device(): pl.pallas_call(functools.partial(kernel, n), out_shape=(jax.ShapeDtypeStr...  74.6 us
    unnamed x2, local copies, waits for them, and re-layouts  2.85 us

profile of v2, /device:TPU:0, one launch (start us, length us, event | category | flops | bytes accessed | tf_op | source)
XLA Modules:
  0.0 78.1 jit_solution(3066034214174463871)
XLA Ops:
  0.6 74.6 %shard_map.104 = (bf16[16,1024]{1,0:T(8,128)(2,1)}, bf16[2,16,1024]{2,1,0:T(8,128)(2,1)}) custom-call(bf16[16,1024]{1,0:T(8,128)(2,1)} %hidden.1, bf16[1024]{0:T(1024)(128)(2,1)} %gain.1, s32[16]{0:T(128)} %lengths.1, bf16[1024,16384]{1,0:T(8,128)(2,1)} %wq.1, bf16[1024,1024]{1,0:T(8,128)(2,1)} %wk.1, bf16[1024,1024]{1,0:T(8,128)(2,1)} %wv.1, ...), custom_call_target="tpu_custom_call" | custom-call | flops 1073741824 | bytes 67108864 | tf_op jit(solution)/shard_map/pallas_call | solution.py:511
  75.2 1.4 %copy.13 = bf16[16,1024]{1,0:T(8,128)(2,1)} copy(bf16[16,1024]{1,0:T(8,128)(2,1)} %get-tuple-element.4) | data formatting | bytes 65536
  76.6 1.5 %copy.14 = bf16[2,16,1024]{2,1,0:T(8,128)(2,1)} copy(bf16[2,16,1024]{2,1,0:T(8,128)(2,1)} %get-tuple-element.5) | data formatting | bytes 131072

commit v3 on v2

--- a/solution.py
+++ b/solution.py
@@ -20,8 +20,8 @@
     n, hidden, gain, lengths, wq, wk, wv, wo, ck, cv,
     out, new,
     wbuf, kvbuf, ckb, cvb, kvp, part, sibr, yr, zr, qg, mixb, sibm, ym, zm, hacc, hg, acc,
-    wsem, kvsem, wosem, csem, s1s, s1r, y1s, y1r, z1s, z1r, gss, gsr, gys, gyr, gzs, gzr,
-    s2s, s2r, y2s, y2r, z2s, z2r, hss, hsr, hys, hyr, hzs, hzr,
+    wsem, kvsem, wosem, csem, s1s, s1r, y1s, y1r, z1s, z1r, gss, gsr, gds, gdr,
+    s2s, s2r, y2s, y2r, z2s, z2r, hss, hsr, hds, hdr,
 ):
     rows, depth = hidden.shape
     width = wbuf.shape[2]
@@ -74,11 +74,15 @@
         pl.semaphore_signal(barrier, inc=1, device_id={"gx": target}, device_id_type=pl.DeviceIdType.MESH)
 
     greet(sibling)
-    greet(across)
-    each_other(lambda p: greet(along(p)))
+
+    def greet_chip(u, carry):
+        greet(2 * lax.rem(chip + u, chips) + core)
+        return carry
+
+    lax.fori_loop(1, chips, greet_chip, 0)
 
     def block(t, second):
-        c = 2 * turn(pair + 1 + t // 2) + lax.rem(side + 1 + t, 2)
+        c = 2 * turn(pair + 1 + t) + lax.rem(side + 1 + t // pairs, 2)
         return c, 2 * c + (core if second else other)
 
     def load_w(t, second):
@@ -119,7 +123,7 @@
     copy_v.wait()
     kvp[:, kv_width:] = jnp.dot(scaled, kvbuf[1], preferred_element_type=F32)
 
-    pl.semaphore_wait(barrier, pairs + 1)
+    pl.semaphore_wait(barrier, chips)
 
     def sib1(c):
         return remote(part.at[2 * c + other], sibr.at[c], s1s.at[c], s1r.at[c], sibling)
@@ -145,8 +149,7 @@
         y1(p).wait_recv()
         part[2 * c + core] = part[2 * c + core] + sibr[c] + yr[p]
 
-    def project_side(i, is_near):
-        t = 2 * i + is_near
+    def project_chip(t):
         for second in range(2):
             c, d = block(t, second)
             load_w(t, second).wait()
@@ -162,8 +165,21 @@
             if not second:
                 sib1(c).start()
 
-    def project(i, carry):
-        project_side(i, 0)
+    def project_far(i, carry):
+        project_chip(i)
+
+        @pl.when(i > 0)
+        def _():
+            finish1_far(turn(pair + i))
+
+        return carry
+
+    def project_near(i, carry):
+        project_chip(pairs + i)
+
+        @pl.when(i == 0)
+        def _():
+            finish1_far(pair)
 
         @pl.when(i > 0)
         def _():
@@ -171,11 +187,10 @@
             finish1_near(before)
             z1(before).start()
 
-        project_side(i, 1)
-        finish1_far(turn(pair + 1 + i))
-        return carry
-
-    lax.fori_loop(0, pairs, project, 0)
+        return carry
+
+    lax.fori_loop(0, pairs, project_far, 0)
+    lax.fori_loop(0, pairs, project_near, 0)
 
     copy_ck = pltpu.make_async_copy(ck, ckb, csem.at[0])
     copy_cv = pltpu.make_async_copy(cv, cvb, csem.at[1])
@@ -213,57 +228,44 @@
     qg[me, :, width:] = (x * cos_key + pltpu.roll(x, half, 1) * (sin_table * is_key)).astype(BF16)
 
     class Spread:
-        def __init__(self, ref, ss, sr, ys, yr_, zs, zr_):
-            self.ref, self.sems = ref, (ss, sr, ys, yr_, zs, zr_)
+        def __init__(self, ref, ss, sr, ds, dr):
+            self.ref, self.ss, self.sr, self.ds, self.dr = ref, ss, sr, ds, dr
 
         def to_sibling(self, c):
-            ss, sr = self.sems[:2]
             at = self.ref.at[2 * c + core]
-            return remote(at, at, ss.at[c], sr.at[c], sibling)
+            return remote(at, at, self.ss.at[c], self.sr.at[c], sibling)
 
         def from_sibling(self, c):
-            ss, sr = self.sems[:2]
             at = self.ref.at[2 * c + other]
-            return remote(at, at, ss.at[c], sr.at[c], sibling)
-
-        def to_across(self, p):
-            ys, yr_ = self.sems[2:4]
-            at = self.ref.at[along(p)]
-            return remote(at, at, ys.at[p], yr_.at[p], across)
-
-        def from_across(self, p):
-            ys, yr_ = self.sems[2:4]
-            at = self.ref.at[2 * far(p) + core]
-            return remote(at, at, ys.at[p], yr_.at[p], across)
-
-        def to_along(self, p):
-            zs, zr_ = self.sems[4:]
+            return remote(at, at, self.ss.at[c], self.sr.at[c], sibling)
+
+        def to_chip(self, c):
             at = self.ref.at[me]
-            return remote(at, at, zs.at[p], zr_.at[pair], along(p))
-
-        def from_along(self, p):
-            zs, zr_ = self.sems[4:]
-            at = self.ref.at[along(p)]
-            return remote(at, at, zs.at[p], zr_.at[p], along(p))
+            return remote(at, at, self.ds.at[c], self.dr.at[chip], 2 * c + core)
+
+        def from_chip(self, c):
+            at = self.ref.at[2 * c + core]
+            return remote(at, at, self.ds.at[c], self.dr.at[c], 2 * c + core)
 
         def begin(self):
-            def send(u, carry):
-                self.to_along(turn(pair + u)).start()
+            self.to_sibling(chip).start()
+
+            def send_far(u, carry):
+                self.to_chip(far(turn(pair + u))).start()
                 return carry
-            lax.fori_loop(1, pairs, send, 0)
-            self.to_across(pair).start()
-            self.to_sibling(chip).start()
-
-        def relay_near(self, p):
-            self.from_along(p).wait_recv()
-            self.to_across(p).start()
-            self.to_sibling(near(p)).start()
-
-        def relay_far(self, p):
-            self.from_across(p).wait_recv()
-            self.to_sibling(far(p)).start()
-
-    spread1 = Spread(qg, gss, gsr, gys, gyr, gzs, gzr)
+
+            def send_near(u, carry):
+                self.to_chip(near(turn(pair + u))).start()
+                return carry
+
+            lax.fori_loop(0, pairs, send_far, 0)
+            lax.fori_loop(1, pairs, send_near, 0)
+
+        def relay(self, c):
+            self.from_chip(c).wait_recv()
+            self.to_sibling(c).start()
+
+    spread1 = Spread(qg, gss, gsr, gds, gdr)
     spread1.begin()
 
     column = lax.broadcasted_iota(jnp.int32, (group * rows, rows * spots), 1)
@@ -342,40 +344,56 @@
         copy_cv.wait()
         spread1.from_sibling(chip).wait_recv()
         attend(chip)
-        spread1.relay_far(pair)
-        spread1.relay_near(turn(pair - 1))
-        spread1.from_sibling(far(pair)).wait_recv()
-        attend(far(pair))
-
-        def of_pair(u, carry):
+        spread1.relay(far(pair))
+
+        def attend_far(u, carry):
             p = turn(pair - u)
-            spread1.relay_far(p)
 
             @pl.when(u + 1 < pairs)
             def _():
-                spread1.relay_near(turn(pair - u - 1))
+                spread1.relay(far(turn(pair - u - 1)))
+
+            @pl.when(u + 1 == pairs)
+            def _():
+                spread1.relay(near(turn(pair - 1)))
 
             spread1.from_sibling(far(p)).wait_recv()
             attend(far(p))
-            finish2_far(turn(p + 1))
+
+            @pl.when(u > 0)
+            def _():
+                finish2_far(turn(p + 1))
+
+            return carry
+
+        def attend_near(u, carry):
+            p = turn(pair - u)
+
+            @pl.when(u + 1 < pairs)
+            def _():
+                spread1.relay(near(turn(pair - u - 1)))
+
             spread1.from_sibling(near(p)).wait_recv()
             attend(near(p))
 
+            @pl.when(u == 1)
+            def _():
+                finish2_far(turn(pair + 1))
+
             @pl.when(u > 1)
             def _():
                 finish2_near(turn(p + 1))
 
             return carry
 
-        lax.fori_loop(1, pairs, of_pair, 0)
-        last = turn(pair + 1)
-        finish2_far(last)
-        finish2_near(last)
+        lax.fori_loop(0, pairs, attend_far, 0)
+        lax.fori_loop(1, pairs, attend_near, 0)
+        finish2_near(turn(pair + 1))
         finish2_near(pair)
     else:
-        each_other(spread1.relay_near)
-        spread1.relay_far(pair)
-        each_other(spread1.relay_far)
+        spread1.relay(far(pair))
+        each_other(lambda p: spread1.relay(far(p)))
+        each_other(lambda p: spread1.relay(near(p)))
         copy_ck.wait()
         copy_cv.wait()
 
@@ -441,7 +459,7 @@
         at = slice(j * HD, (j + 1) * HD)
         hg[me, :, at] = (hacc[:, at] / total[:, j:j + 1]).astype(BF16)
 
-    spread2 = Spread(hg, hss, hsr, hys, hyr, hzs, hzr)
+    spread2 = Spread(hg, hss, hsr, hds, hdr)
     spread2.begin()
 
     def product(d):
@@ -450,26 +468,34 @@
 
     acc[...] = jnp.zeros_like(acc)
     product(me)
-    spread2.relay_far(pair)
     spread2.from_sibling(chip).wait_recv()
     product(sibling)
 
-    def project_out(p):
-        spread2.relay_near(p)
-        before = turn(p + 1)
-        product(2 * far(before) + core)
-        spread2.from_sibling(far(before)).wait_recv()
-        product(2 * far(before) + other)
-        spread2.relay_far(p)
-        product(along(p))
-        spread2.from_sibling(near(p)).wait_recv()
-        product(2 * near(p) + other)
-
-    each_other(project_out)
-    last = turn(pair + 1)
-    product(2 * far(last) + core)
-    spread2.from_sibling(far(last)).wait_recv()
-    product(2 * far(last) + other)
+    def project_out(c, before, first):
+        spread2.relay(c)
+        if not first:
+            spread2.from_sibling(before).wait_recv()
+            product(2 * before + other)
+        product(2 * c + core)
+
+    def out_far(u, carry):
+        p = turn(pair - u)
+        project_out(far(p), far(turn(p + 1)), False)
+        return carry
+
+    def out_near(u, carry):
+        p = turn(pair - u)
+        project_out(near(p), near(turn(p + 1)), False)
+        return carry
+
+    project_out(far(pair), chip, True)
+    lax.fori_loop(1, pairs, out_far, 0)
+    last = far(turn(pair + 1))
+    project_out(near(turn(pair - 1)), last, False)
+    lax.fori_loop(2, pairs, out_near, 0)
+    last = near(turn(pair + 1))
+    spread2.from_sibling(last).wait_recv()
+    product(2 * last + other)
     out[...] = acc[...].astype(BF16)
 
     def drain_chip(c, carry):
@@ -482,15 +508,15 @@
     def drain_pair(p, carry):
         y1(p).wait_send()
         y2(p).wait_send()
-        spread1.to_across(p).wait_send()
-        spread2.to_across(p).wait_send()
+        spread1.to_chip(far(p)).wait_send()
+        spread2.to_chip(far(p)).wait_send()
         return carry
 
     def drain_along(p):
         z1(p).wait_send()
         z2(p).wait_send()
-        spread1.to_along(p).wait_send()
-        spread2.to_along(p).wait_send()
+        spread1.to_chip(near(p)).wait_send()
+        spread2.to_chip(near(p)).wait_send()
 
     lax.fori_loop(0, chips, drain_chip, 0)
     lax.fori_loop(0, pairs, drain_pair, 0)
@@ -535,7 +561,7 @@
             pltpu.VMEM((n, rows, width), BF16),
             pltpu.VMEM((rows, out_width), F32),
             dma((n,)), dma((2,)), dma((n,)), dma((2,)),
-        ] + [dma((size,)) for size in (chips, chips, pairs, pairs, pairs, pairs) * 4],
+        ] + [dma((size,)) for size in (chips, chips, pairs, pairs, pairs, pairs, chips, chips, chips, chips) * 2],
         compiler_params=pltpu.CompilerParams(
             collective_id=0, has_side_effects=True, vmem_limit_bytes=60 * 1024 * 1024),
         cost_estimate=pl.CostEstimate(

time: 78.4 us -> 63.4 us (0.81)
  Pallas kernels: 74.6 us -> 59.6 us
    pallas_call x1, Pallas kernels: 74.6 us -> 59.6 us  [on_device(): pl.pallas_call(functools.partial(kernel, n), out_shape=(jax.ShapeDtypeStr...]
where the time goes in v3:
time: 63.4 us; the launch traced here: 63.1 us
  Pallas kernels  59.6 us (94%)
  local copies, waits for them, and re-layouts  2.85 us (4%)
  between operations  0.64 us (1%)
    pallas_call x1, Pallas kernels, on_device(): pl.pallas_call(functools.partial(kernel, n), out_shape=(jax.ShapeDtypeStr...  59.6 us
    unnamed x2, local copies, waits for them, and re-layouts  2.85 us

profile of v3, /device:TPU:0, one launch (start us, length us, event | category | flops | bytes accessed | tf_op | source)
XLA Modules:
  0.0 63.1 jit_solution(12143531759129953532)
XLA Ops:
  0.6 59.6 %shard_map.104 = (bf16[16,1024]{1,0:T(8,128)(2,1)}, bf16[2,16,1024]{2,1,0:T(8,128)(2,1)}) custom-call(bf16[16,1024]{1,0:T(8,128)(2,1)} %hidden.1, bf16[1024]{0:T(1024)(128)(2,1)} %gain.1, s32[16]{0:T(128)} %lengths.1, bf16[1024,16384]{1,0:T(8,128)(2,1)} %wq.1, bf16[1024,1024]{1,0:T(8,128)(2,1)} %wk.1, bf16[1024,1024]{1,0:T(8,128)(2,1)} %wv.1, ...), custom_call_target="tpu_custom_call" | custom-call | flops 1073741824 | bytes 67108864 | tf_op jit(solution)/shard_map/pallas_call | solution.py:537
  60.3 1.4 %copy.13 = bf16[16,1024]{1,0:T(8,128)(2,1)} copy(bf16[16,1024]{1,0:T(8,128)(2,1)} %get-tuple-element.4) | data formatting | bytes 65536
  61.6 1.5 %copy.14 = bf16[2,16,1024]{2,1,0:T(8,128)(2,1)} copy(bf16[2,16,1024]{2,1,0:T(8,128)(2,1)} %get-tuple-element.5) | data formatting | bytes 131072

commit v4 on v3

--- a/solution.py
+++ b/solution.py
@@ -149,7 +149,7 @@
         y1(p).wait_recv()
         part[2 * c + core] = part[2 * c + core] + sibr[c] + yr[p]
 
-    def project_chip(t):
+    def project_chip(t, between):
         for second in range(2):
             c, d = block(t, second)
             load_w(t, second).wait()
@@ -164,29 +164,30 @@
 
             if not second:
                 sib1(c).start()
+                between()
 
     def project_far(i, carry):
-        project_chip(i)
-
-        @pl.when(i > 0)
-        def _():
-            finish1_far(turn(pair + i))
-
+        def between():
+            @pl.when(i > 0)
+            def _():
+                finish1_far(turn(pair + i))
+
+        project_chip(i, between)
         return carry
 
     def project_near(i, carry):
-        project_chip(pairs + i)
-
-        @pl.when(i == 0)
-        def _():
-            finish1_far(pair)
-
-        @pl.when(i > 0)
-        def _():
-            before = turn(pair + i)
-            finish1_near(before)
-            z1(before).start()
-
+        def between():
+            @pl.when(i == 0)
+            def _():
+                finish1_far(pair)
+
+            @pl.when(i > 0)
+            def _():
+                before = turn(pair + i)
+                finish1_near(before)
+                z1(before).start()
+
+        project_chip(pairs + i, between)
         return carry
 
     lax.fori_loop(0, pairs, project_far, 0)
@@ -523,6 +524,17 @@
     each_other(drain_along)
 
 
+def place(first, second, first_out, second_out, sem):
+    copies = [
+        pltpu.make_async_copy(first, first_out, sem.at[0]),
+        pltpu.make_async_copy(second, second_out, sem.at[1]),
+    ]
+    for copy in copies:
+        copy.start()
+    for copy in copies:
+        copy.wait()
+
+
 def on_device(hidden, norm_gain, w_query, w_key, w_value, w_out, cache_keys, cache_values, lengths):
     n = lax.axis_size("gx")
     rows, depth = hidden.shape
@@ -534,7 +546,7 @@
     vmem = pl.BlockSpec(memory_space=pltpu.VMEM)
     hbm = pl.BlockSpec(memory_space=pl.ANY)
     dma = pltpu.SemaphoreType.DMA
-    return pl.pallas_call(
+    results = pl.pallas_call(
         functools.partial(kernel, n),
         out_shape=(
             jax.ShapeDtypeStruct((rows, out_width), BF16),
@@ -570,6 +582,14 @@
         hidden, norm_gain, lengths, w_query, w_key, w_value, w_out,
         cache_keys.reshape(rows * spots, kv_width), cache_values.reshape(rows * spots, kv_width),
     )
+    return pl.pallas_call(
+        place,
+        out_shape=tuple(jax.ShapeDtypeStruct(r.shape, r.dtype) for r in results),
+        in_specs=[hbm] * 2,
+        out_specs=(hbm, hbm),
+        scratch_shapes=[dma((2,))],
+        compiler_params=pltpu.CompilerParams(vmem_limit_bytes=60 * 1024 * 1024),
+    )(*results)
 
 
 def solution(mesh):

time: 63.4 us -> 64.9 us (1.024)
  Pallas kernels: 59.6 us -> 64 us
  local copies, waits for them, and re-layouts: 2.85 us -> 0 us
    pallas_call x0 -> x1, Pallas kernels: none -> 4.1 us  [on_device(): pl.pallas_call(place, out_shape=tuple((jax.ShapeDtypeStruct(r.shape, r.dt...]
    unnamed x2 -> x0, local copies, waits for them, and re-layouts: 2.85 us -> none
where the time goes in v4:
time: 64.9 us; the launch traced here: 64.7 us
  Pallas kernels  64 us (99%)
    pallas_call x1, Pallas kernels, on_device(): pl.pallas_call(functools.partial(kernel, n), out_shape=(jax.ShapeDtypeStr...  59.9 us
    pallas_call x1, Pallas kernels, on_device(): pl.pallas_call(place, out_shape=tuple((jax.ShapeDtypeStruct(r.shape, r.dt...  4.1 us

profile of v4, /device:TPU:0, one launch (start us, length us, event | category | flops | bytes accessed | tf_op | source)
XLA Modules:
  0.0 64.7 jit_solution(2937894550724370723)
XLA Ops:
  0.6 59.9 %shard_map.104 = (bf16[16,1024]{1,0:T(8,128)(2,1)}, bf16[2,16,1024]{2,1,0:T(8,128)(2,1)}) custom-call(bf16[16,1024]{1,0:T(8,128)(2,1)} %hidden.1, bf16[1024]{0:T(1024)(128)(2,1)} %gain.1, s32[16]{0:T(128)} %lengths.1, bf16[1024,16384]{1,0:T(8,128)(2,1)} %wq.1, bf16[1024,1024]{1,0:T(8,128)(2,1)} %wk.1, bf16[1024,1024]{1,0:T(8,128)(2,1)} %wv.1, ...), custom_call_target="tpu_custom_call" | custom-call | flops 1073741824 | bytes 67108864 | tf_op jit(solution)/shard_map/pallas_call | solution.py:549
  60.6 4.1 %shard_map.105 = (bf16[16,1024]{1,0:T(8,128)(2,1)}, bf16[2,16,1024]{2,1,0:T(8,128)(2,1)}) custom-call(bf16[16,1024]{1,0:T(8,128)(2,1)} %get-tuple-element.4.first, bf16[2,16,1024]{2,1,0:T(8,128)(2,1)} %get-tuple-element.5.second), custom_call_target="tpu_custom_call" | custom-call | tf_op jit(solution)/shard_map/pallas_call | solution.py:585
